TPU v7x, 32 devices: a whole 2x2x4 slice. The times are simulated.
32 devices in a mesh: seq: 16 (over z, y, core), head: 2 (over x).
Axes of the slice: x: 2, y: 2, z: 4, core: 2. Of those that a mesh axis runs over, the one named last changes fastest.
Arguments:
- queries: bfloat16 [2048, 3072], P(('seq', 'head')), may hold values from -6 to 6
- keys: bfloat16 [2048, 3072], P(('seq', 'head')), may hold values from -6 to 6
- values: bfloat16 [2048, 3072], P(('seq', 'head')), may hold values from -6 to 6
- counts: int32 [4], replicated, may hold values from 256 to 512, as said below
- plan: int32 [4], replicated, may hold values from 0 to 7
- group_mask: int32 [4, 4], replicated, may hold values from 0 to 1, as said below
- gate_table: float32 [8, 3072], replicated, may hold values from -6 to 6
Outputs:
- attended: bfloat16 [2048, 3072], P(('seq', 'head'))
Inputs may be any that keep to these rules, and one draw needn't show every extreme that they name: `counts`: every group's count is at least half of 512; some group is full. `group_mask`: the diagonal is 1 and every entry above it is 0.
All inputs are finite; a program needn't handle non-finite values.
Results may differ from a plain program's by a relative error of at most 0.0046.
Values may be sent and summed in bfloat16 or wider, within the bound.
No kernel may reach another device: no remote copies, remote signals or barrier semaphores. Data moves between devices by JAX's collectives and lax.ppermute only.
A program may use at most 128 MiB of HBM per device.

v0:
```python
import functools
import math

import jax
import jax.numpy as jnp
from jax import lax
from jax.experimental import pallas as pl
from jax.experimental.pallas import tpu as pltpu
from jax.sharding import PartitionSpec as P

HEAD_DIM = 128
GROUPS = 4
LEVELS = 8


def lookup(table, index):
    hits = index[:, None] == jnp.arange(table.shape[0], dtype=jnp.int32)[None, :]
    return jnp.sum(jnp.where(hits, table[None, :], 0), axis=1)


def attend(
    work_q, k_local, v_local, row_group, row_pos, counts, plan, group_mask, gate_slice, group_tok
):
    rows = work_q.shape[0]
    width = work_q.shape[1]
    heads_here = width // HEAD_DIM
    scale = 1.0 / math.sqrt(HEAD_DIM)
    q_three = work_q.reshape(rows, heads_here, HEAD_DIM)
    row_onehot = (row_group[:, None] == jnp.arange(GROUPS, dtype=jnp.int32)[None, :]).astype(
        jnp.float32
    )
    mask_rows = jnp.dot(row_onehot, group_mask.astype(jnp.float32))
    k_piece = lax.all_gather(k_local, "seq", axis=0, tiled=True)
    v_piece = lax.all_gather(v_local, "seq", axis=0, tiled=True)
    count = k_piece.shape[0]
    index = jnp.arange(count, dtype=jnp.int32)
    k_group = index // group_tok
    k_pos = index % group_tok
    k_onehot = (k_group[:, None] == jnp.arange(GROUPS, dtype=jnp.int32)[None, :]).astype(
        jnp.float32
    )
    k_valid = k_pos < lookup(counts, k_group)
    allowed = (jnp.dot(mask_rows, k_onehot.T) > 0.5) & k_valid[None, :]
    running = jnp.full((heads_here, rows), -1e30, jnp.float32)
    k_three = k_piece.reshape(count, heads_here, HEAD_DIM)
    v_three = v_piece.reshape(count, heads_here, HEAD_DIM)
    scores = (
        jnp.einsum("qhd,khd->hqk", q_three, k_three, preferred_element_type=jnp.float32) * scale
    )
    scores = jnp.where(allowed[None], scores, jnp.float32(-1e30))
    newest = jnp.maximum(running, jnp.max(scores, axis=2))
    weights = jnp.exp(scores - newest[:, :, None]) * allowed[None].astype(jnp.float32)
    total = jnp.sum(weights, axis=2)
    rounded = weights.astype(jnp.bfloat16)
    accum = jnp.einsum("hqk,khd->hqd", rounded, v_three, preferred_element_type=jnp.float32)
    running, total, accum = (newest, total, accum)
    mixed = accum / total[:, :, None]
    mixed = jnp.transpose(mixed, (1, 0, 2)).reshape(rows, width)
    level_rows = lookup(plan, row_group)
    level_hits = level_rows[:, None] == jnp.arange(LEVELS, dtype=jnp.int32)[None, :]
    gates = jnp.sum(
        jnp.where(level_hits[:, :, None], gate_slice[None, :, :], jnp.float32(0.0)), axis=1
    )
    live = row_pos < lookup(counts, row_group)
    return jnp.where(live[:, None], mixed * gates, jnp.float32(0.0)).astype(jnp.bfloat16)


def gathered(queries, keys, values, counts, plan, group_mask, gate_table):
    n_seq = lax.axis_size("seq")
    n_head = lax.axis_size("head")
    per_group = n_seq // GROUPS
    tok_dev = queries.shape[0] * n_head
    group_tok = tok_dev * per_group
    q_local, k_local, v_local = (
        lax.all_to_all(queries, "head", split_axis=1, concat_axis=0, tiled=True),
        lax.all_to_all(keys, "head", split_axis=1, concat_axis=0, tiled=True),
        lax.all_to_all(values, "head", split_axis=1, concat_axis=0, tiled=True),
    )
    width = q_local.shape[1]
    seq_index = lax.axis_index("seq")
    own_group = seq_index // per_group
    positions = seq_index % per_group * tok_dev + jnp.arange(tok_dev, dtype=jnp.int32)
    gate_slice = lax.dynamic_slice_in_dim(gate_table, lax.axis_index("head") * width, width, 1)
    row_group = jnp.full((tok_dev,), own_group, jnp.int32)
    result = attend(
        q_local,
        k_local,
        v_local,
        row_group,
        positions,
        counts,
        plan,
        group_mask,
        gate_slice,
        group_tok,
    )
    return lax.all_to_all(result, "head", split_axis=0, concat_axis=1, tiled=True)


def pack_kernel(parts, held, *refs):
    count = (len(refs) - 2) // 2
    in_refs, out_ref, bufs, sems = refs[:count], refs[count], refs[count + 1 : -1], refs[-1]
    slots = out_ref.shape[0] // parts
    copies = [pltpu.make_async_copy(in_refs[i], bufs[i], sems.at[i]) for i in range(count)]
    for copy in copies:
        copy.start()
    for s in range(held, slots):
        for p in range(parts):
            out_ref[p * slots + s] = jnp.zeros(out_ref.shape[1:], out_ref.dtype)
    for i, copy in enumerate(copies):
        copy.wait()
        for p in range(parts):
            for s in range(held):
                h = p * held + s
                out_ref[p * slots + s, i] = bufs[i][:, h * HEAD_DIM : (h + 1) * HEAD_DIM]


def pack(arrays, parts, held, n_dev):
    local, feat = arrays[0].shape
    count = len(arrays)
    return pl.pallas_call(
        functools.partial(pack_kernel, parts, held),
        out_shape=jax.ShapeDtypeStruct((n_dev, count, local, HEAD_DIM), jnp.bfloat16),
        in_specs=[pl.BlockSpec(memory_space=pl.ANY)] * count,
        out_specs=pl.BlockSpec(memory_space=pltpu.VMEM),
        scratch_shapes=[pltpu.VMEM((local, feat), jnp.bfloat16)] * count + [pltpu.SemaphoreType.DMA((count,))],
        compiler_params=pltpu.CompilerParams(vmem_limit_bytes=60 * 1024 * 1024),
        cost_estimate=pl.CostEstimate(flops=0, bytes_accessed=count * local * feat * 5, transcendentals=0),
        name="pack",
    )(*arrays)


def unpack_kernel(parts, held, in_ref, out_ref, sem):
    slots = in_ref.shape[0] // parts
    for p in range(parts):
        for s in range(held):
            h = p * held + s
            pltpu.make_async_copy(
                in_ref.at[p * slots + s], out_ref.at[:, h * HEAD_DIM : (h + 1) * HEAD_DIM], sem
            ).start()
    pltpu.make_async_copy(out_ref, out_ref, sem).wait()


def attention_kernel(
    counts_ref, plan_ref, mask_ref, place_ref, got_ref, gate_ref, out_ref, bias_ref, score_ref, top_ref, mixed_ref
):
    n_dev, _, local, _ = got_ref.shape
    per_group = n_dev // GROUPS
    rows = per_group * local
    factor = 1.0 / math.sqrt(HEAD_DIM)
    head = place_ref[0]
    busy = place_ref[1]

    @pl.when(busy == 1)
    def _():
        gates = gate_ref[:, pl.ds(pl.multiple_of(head * HEAD_DIM, HEAD_DIM), HEAD_DIM)]
        level = lax.broadcasted_iota(jnp.int32, (LEVELS, HEAD_DIM), 0)
        place = lax.broadcasted_iota(jnp.int32, (rows, HEAD_DIM), 0)
        lane = lax.broadcasted_iota(jnp.int32, (rows, HEAD_DIM), 1)
        one = jnp.where(lane == 0, 1.0, 0.0).astype(jnp.bfloat16)
        ones = jnp.ones((rows, HEAD_DIM), jnp.bfloat16)

        def part(group, kind):
            return got_ref[pl.ds(group * per_group, per_group), kind].reshape(rows, HEAD_DIM)

        def score(c, d):
            return lax.dot_general(
                jnp.concatenate([part(c, 0), one], axis=1),
                jnp.concatenate([part(d, 1), bias_ref[d]], axis=1),
                (((1,), (1,)), ((), ())),
                preferred_element_type=jnp.float32,
            )

        def lane_top(scores, top):
            pieces = [scores[:, i : i + HEAD_DIM] for i in range(0, rows, HEAD_DIM)]
            return functools.reduce(jnp.maximum, pieces, top)

        def product(scores, top, d):
            shift = jnp.concatenate([top] * (rows // HEAD_DIM), axis=1)
            weights = jnp.exp(scores * factor - shift).astype(jnp.bfloat16)
            return jnp.dot(
                weights, jnp.concatenate([part(d, 2), ones], axis=1), preferred_element_type=jnp.float32
            )

        @pl.loop(0, GROUPS)
        def _(c):
            bias_ref[c] = jnp.where(place < counts_ref[c], 0.0, -1e30).astype(jnp.bfloat16)
            top_ref[...] = jnp.full(top_ref.shape, -1e30, jnp.float32)

            @pl.loop(0, c)
            def _(d):
                @pl.when(mask_ref[c, d] == 1)
                def _():
                    scores = score(c, d)
                    score_ref[d] = scores
                    top_ref[...] = lane_top(scores, top_ref[...])

            own = score(c, c)
            top = jnp.max(lane_top(own, top_ref[...]), axis=1, keepdims=True) * factor
            top = jnp.broadcast_to(top, top_ref.shape)
            top_ref[...] = top
            mixed_ref[...] = product(own, top, c)

            @pl.loop(0, c)
            def _(d):
                @pl.when(mask_ref[c, d] == 1)
                def _():
                    mixed_ref[...] += product(score_ref[d], top_ref[...], d)

            gate = jnp.sum(jnp.where(level == plan_ref[c], gates, jnp.float32(0.0)), axis=0, keepdims=True)
            mixed = mixed_ref[:, :HEAD_DIM] / mixed_ref[:, HEAD_DIM:] * gate
            mixed = jnp.where(place < counts_ref[c], mixed, jnp.float32(0.0))
            out_ref[pl.ds(c * per_group, per_group)] = mixed.astype(jnp.bfloat16).reshape(
                per_group, local, HEAD_DIM
            )

    @pl.when(busy == 0)
    def _():
        out_ref[...] = jnp.zeros_like(out_ref)


def head_each(queries, keys, values, counts, plan, group_mask, gate_table):
    axes = ("seq", "head")
    n_dev = lax.axis_size("seq") * lax.axis_size("head")
    local, feat = queries.shape
    heads = feat // HEAD_DIM
    parts = math.gcd(heads, n_dev)
    held, slots = heads // parts, n_dev // parts
    index = lax.axis_index("seq") * lax.axis_size("head") + lax.axis_index("head")
    lane = index % slots
    busy = (lane < held).astype(jnp.int32)
    head = jnp.minimum(index // slots * held + lane, heads - 1)
    place = jnp.stack([head, busy]).astype(jnp.int32)
    smem = pl.BlockSpec(memory_space=pltpu.SMEM)
    vmem = pl.BlockSpec(memory_space=pltpu.VMEM)

    sent = pack((queries, keys, values), parts, held, n_dev)
    got = lax.all_to_all(sent, axes, split_axis=0, concat_axis=0, tiled=True)
    rows = n_dev * local // GROUPS
    result = pl.pallas_call(
        attention_kernel,
        out_shape=jax.ShapeDtypeStruct((n_dev, local, HEAD_DIM), jnp.bfloat16),
        in_specs=[smem, smem, smem, smem, vmem, vmem],
        out_specs=vmem,
        scratch_shapes=[
            pltpu.VMEM((GROUPS, rows, HEAD_DIM), jnp.bfloat16),
            pltpu.VMEM((GROUPS - 1, rows, rows), jnp.float32),
            pltpu.VMEM((rows, HEAD_DIM), jnp.float32),
            pltpu.VMEM((rows, 2 * HEAD_DIM), jnp.float32),
        ],
        compiler_params=pltpu.CompilerParams(vmem_limit_bytes=40 * 1024 * 1024),
        name="attention",
    )(counts, plan, group_mask, place, got, gate_table)
    back = lax.all_to_all(result, axes, split_axis=0, concat_axis=0, tiled=True)
    return pl.pallas_call(
        functools.partial(unpack_kernel, parts, held),
        out_shape=jax.ShapeDtypeStruct((local, feat), jnp.bfloat16),
        in_specs=[vmem],
        out_specs=pl.BlockSpec(memory_space=pl.ANY),
        scratch_shapes=[pltpu.SemaphoreType.DMA],
        compiler_params=pltpu.CompilerParams(vmem_limit_bytes=16 * 1024 * 1024),
        name="unpack",
    )(back)


def on_device(queries, keys, values, counts, plan, group_mask, gate_table):
    n_dev = lax.axis_size("seq") * lax.axis_size("head")
    heads = queries.shape[1] // HEAD_DIM
    plan_of = head_each if heads <= n_dev <= 2 * heads else gathered
    return plan_of(queries, keys, values, counts, plan, group_mask, gate_table)


def solution(mesh):
    in_specs = (
        P(("seq", "head"), None),
        P(("seq", "head"), None),
        P(("seq", "head"), None),
        P(),
        P(),
        P(),
        P(),
    )
    out_specs = P(("seq", "head"), None)
    return jax.shard_map(
        on_device, mesh=mesh, in_specs=in_specs, out_specs=out_specs, check_vma=False
    )
```

profile of v0, /device:TPU:1, one launch (start us, length us, event | category | flops | bytes accessed | tf_op | source)
XLA Modules:
  0.0 75.6 jit_solution(13147745595658683653)
XLA Ops:
  0.0 2.5 %pack.1 = bf16[32,3,64,128]{3,2,1,0:T(8,128)(2,1)} custom-call(bf16[64,3072]{1,0:T(8,128)(2,1)} %refs_0_.1, bf16[64,3072]{1,0:T(8,128)(2,1)} %refs_1_.1, bf16[64,3072]{1,0:T(8,128)(2,1)} %refs_2_.1), custom_call_target="tpu_custom_call" | custom-call | bytes 2949120 | tf_op jit(solution)/shard_map/pack/pallas_call | solution.py:121
  2.5 0.0 copy-start
  2.5 0.0 copy-start.1
  2.5 0.0 copy-start.2
  2.5 0.0 copy-start.3
  2.5 7.1 %all-to-all-start = ((bf16[32,3,64,128]{3,2,1,0:T(8,128)(2,1)}), bf16[32,3,64,128]{3,2,1,0:T(8,128)(2,1)S(1)}, u32[]{:S(2)}, u32[]{:S(2)}) async-start(bf16[32,3,64,128]{3,2,1,0:T(8,128)(2,1)} %pack.1), calls=%async_computation | async-start | bytes 3145728 | tf_op jit(solution)/shard_map/all_to_all | solution.py:238
  9.7 0.1 pad_add_fusion.place_ref
  9.8 36.8 %all-to-all-done.got_ref = bf16[32,3,64,128]{3,2,1,0:T(8,128)(2,1)S(1)} async-done(((bf16[32,3,64,128]{3,2,1,0:T(8,128)(2,1)}), bf16[32,3,64,128]{3,2,1,0:T(8,128)(2,1)S(1)}, u32[]{:S(2)}, u32[]{:S(2)}) %all-to-all-start) | async-done | bytes 1572896 | tf_op jit(solution)/shard_map/all_to_all | solution.py:238
  46.5 0.0 copy-done
  46.5 0.0 copy-done.1
  46.5 0.0 copy-done.2
  46.5 0.0 copy-done.3
  46.5 8.4 %attention.1 = bf16[32,64,128]{2,1,0:T(8,128)(2,1)S(1)} custom-call(s32[4]{0:T(128)S(1)} %copy-done.2, s32[4]{0:T(128)S(1)} %copy-done.3, s32[4,4]{1,0:T(4,128)S(1)} %copy-done.1, s32[2]{0:T(128)S(1)} %pad_add_fusion.place_ref, bf16[32,3,64,128]{3,2,1,0:T(8,128)(2,1)S(1)} %all-to-all-done.got_ref, f32[8,3072]{1,0:T(8,128)S(1)} %copy-done), custom_call_target="tpu_custom_call" | custom-call | tf_op jit(solution)/shard_map/attention/pallas_call | solution.py:240
  55.0 19.9 %all_to_all.10.in_ref = bf16[32,64,128]{2,1,0:T(8,128)(2,1)S(1)} all-to-all(bf16[32,64,128]{2,1,0:T(8,128)(2,1)S(1)} %attention.1), channel_id=1, replica_groups=mesh['seq'=16,'head'=2] {'seq','head'}, dimensions={0} | all-to-all | bytes 1048576 | tf_op jit(solution)/shard_map/all_to_all | solution.py:254
  74.9 0.7 unpack.1
Async XLA Ops:
  2.5 44.0 %copy-start = (f32[8,3072]{1,0:T(8,128)S(1)}, f32[8,3072]{1,0:T(8,128)}, u32[]{:S(2)}) copy-start(f32[8,3072]{1,0:T(8,128)} %gate_ref.1) | copy-start | bytes 294916
  2.5 44.0 %copy-start.1 = (s32[4,4]{1,0:T(4,128)S(1)}, s32[4,4]{1,0:T(4,128)}, u32[]{:S(2)}) copy-start(s32[4,4]{1,0:T(4,128)} %mask_ref.1) | copy-start | bytes 196
  2.5 44.0 %copy-start.2 = (s32[4]{0:T(128)S(1)}, s32[4]{0:T(128)}, u32[]{:S(2)}) copy-start(s32[4]{0:T(128)} %counts_ref.1) | copy-start | bytes 52
  2.5 44.0 %copy-start.3 = (s32[4]{0:T(128)S(1)}, s32[4]{0:T(128)}, u32[]{:S(2)}) copy-start(s32[4]{0:T(128)} %plan_ref.1) | copy-start | bytes 52
  2.5 44.0 %all-to-all-start = ((bf16[32,3,64,128]{3,2,1,0:T(8,128)(2,1)}), bf16[32,3,64,128]{3,2,1,0:T(8,128)(2,1)S(1)}, u32[]{:S(2)}, u32[]{:S(2)}) async-start(bf16[32,3,64,128]{3,2,1,0:T(8,128)(2,1)} %pack.1), calls=%async_computation | async-start | bytes 3145728 | tf_op jit(solution)/shard_map/all_to_all | solution.py:238
where the time goes:
time: 75.5 us; the launch traced here: 75.6 us
  waiting for transfers between devices  36.8 us (49%)
  blocking collectives  19.9 us (26%)
  Pallas kernels  11.7 us (15%)
  starting transfers between devices  7.1 us (9%)
    all_to_all x1, waiting for transfers between devices, head_each(): got = lax.all_to_all(sent, axes, split_axis=0, concat_axis=0, tiled=True)  36.8 us
    all_to_all x1, blocking collectives, head_each(): back = lax.all_to_all(result, axes, split_axis=0, concat_axis=0, tiled=True)  19.9 us
    pallas_call x1, Pallas kernels, head_each(): pl.pallas_call(attention_kernel, out_shape=jax.ShapeDtypeStruct((n_dev, l...  8.44 us
    all_to_all x1, starting transfers between devices, head_each(): got = lax.all_to_all(sent, axes, split_axis=0, concat_axis=0, tiled=True)  7.1 us
    pallas_call x1, Pallas kernels, pack(): pl.pallas_call(functools.partial(pack_kernel, parts, held), out_shape=jax...  2.48 us
  transfers between devices with their start and end apart: 1, of which 1 were waited for; matrix products, arithmetic and copies ran while one was open for 0% of the time, Pallas kernels for 0%

commit v1 on v0

--- a/solution.py
+++ b/solution.py
@@ -97,22 +97,27 @@
     return lax.all_to_all(result, "head", split_axis=0, concat_axis=1, tiled=True)
 
 
-def pack_kernel(parts, held, *refs):
-    count = (len(refs) - 2) // 2
-    in_refs, out_ref, bufs, sems = refs[:count], refs[count], refs[count + 1 : -1], refs[-1]
+def pack_kernel(parts, held, q_ref, k_ref, v_ref, out_ref, in_buf, out_buf, in_sem, out_sem):
     slots = out_ref.shape[0] // parts
-    copies = [pltpu.make_async_copy(in_refs[i], bufs[i], sems.at[i]) for i in range(count)]
+    arrays = (q_ref, k_ref, v_ref)
+    copies = [pltpu.make_async_copy(ref, in_buf.at[i], in_sem.at[i]) for i, ref in enumerate(arrays)]
     for copy in copies:
         copy.start()
     for s in range(held, slots):
         for p in range(parts):
-            out_ref[p * slots + s] = jnp.zeros(out_ref.shape[1:], out_ref.dtype)
+            for i in range(len(arrays)):
+                out_buf[i, p * slots + s] = jnp.zeros(out_buf.shape[2:], out_buf.dtype)
+    stores = []
     for i, copy in enumerate(copies):
         copy.wait()
         for p in range(parts):
             for s in range(held):
                 h = p * held + s
-                out_ref[p * slots + s, i] = bufs[i][:, h * HEAD_DIM : (h + 1) * HEAD_DIM]
+                out_buf[i, p * slots + s] = in_buf[i, :, h * HEAD_DIM : (h + 1) * HEAD_DIM]
+        stores.append(pltpu.make_async_copy(out_buf.at[i], out_ref.at[:, i], out_sem.at[i]))
+        stores[-1].start()
+    for store in stores:
+        store.wait()
 
 
 def pack(arrays, parts, held, n_dev):
@@ -122,10 +127,14 @@
         functools.partial(pack_kernel, parts, held),
         out_shape=jax.ShapeDtypeStruct((n_dev, count, local, HEAD_DIM), jnp.bfloat16),
         in_specs=[pl.BlockSpec(memory_space=pl.ANY)] * count,
-        out_specs=pl.BlockSpec(memory_space=pltpu.VMEM),
-        scratch_shapes=[pltpu.VMEM((local, feat), jnp.bfloat16)] * count + [pltpu.SemaphoreType.DMA((count,))],
+        out_specs=pl.BlockSpec(memory_space=pl.ANY),
+        scratch_shapes=[
+            pltpu.VMEM((count, local, feat), jnp.bfloat16),
+            pltpu.VMEM((count, n_dev, local, HEAD_DIM), jnp.bfloat16),
+            pltpu.SemaphoreType.DMA((count,)),
+            pltpu.SemaphoreType.DMA((count,)),
+        ],
         compiler_params=pltpu.CompilerParams(vmem_limit_bytes=60 * 1024 * 1024),
-        cost_estimate=pl.CostEstimate(flops=0, bytes_accessed=count * local * feat * 5, transcendentals=0),
         name="pack",
     )(*arrays)
 
@@ -142,14 +151,23 @@
 
 
 def attention_kernel(
-    counts_ref, plan_ref, mask_ref, place_ref, got_ref, gate_ref, out_ref, bias_ref, score_ref, top_ref, mixed_ref
+    info_ref, got_ref, gate_ref, out_ref, bias_ref, score_ref, top_ref, mixed_ref
 ):
     n_dev, _, local, _ = got_ref.shape
     per_group = n_dev // GROUPS
     rows = per_group * local
     factor = 1.0 / math.sqrt(HEAD_DIM)
-    head = place_ref[0]
-    busy = place_ref[1]
+    head = info_ref[0]
+    busy = info_ref[1]
+
+    def count_of(group):
+        return info_ref[2 + group]
+
+    def level_of(group):
+        return info_ref[2 + GROUPS + group]
+
+    def sees(group, other):
+        return info_ref[2 + 2 * GROUPS + group * GROUPS + other] == 1
 
     @pl.when(busy == 1)
     def _():
@@ -184,12 +202,12 @@
 
         @pl.loop(0, GROUPS)
         def _(c):
-            bias_ref[c] = jnp.where(place < counts_ref[c], 0.0, -1e30).astype(jnp.bfloat16)
+            bias_ref[c] = jnp.where(place < count_of(c), 0.0, -1e30).astype(jnp.bfloat16)
             top_ref[...] = jnp.full(top_ref.shape, -1e30, jnp.float32)
 
             @pl.loop(0, c)
             def _(d):
-                @pl.when(mask_ref[c, d] == 1)
+                @pl.when(sees(c, d))
                 def _():
                     scores = score(c, d)
                     score_ref[d] = scores
@@ -203,13 +221,13 @@
 
             @pl.loop(0, c)
             def _(d):
-                @pl.when(mask_ref[c, d] == 1)
+                @pl.when(sees(c, d))
                 def _():
                     mixed_ref[...] += product(score_ref[d], top_ref[...], d)
 
-            gate = jnp.sum(jnp.where(level == plan_ref[c], gates, jnp.float32(0.0)), axis=0, keepdims=True)
+            gate = jnp.sum(jnp.where(level == level_of(c), gates, jnp.float32(0.0)), axis=0, keepdims=True)
             mixed = mixed_ref[:, :HEAD_DIM] / mixed_ref[:, HEAD_DIM:] * gate
-            mixed = jnp.where(place < counts_ref[c], mixed, jnp.float32(0.0))
+            mixed = jnp.where(place < count_of(c), mixed, jnp.float32(0.0))
             out_ref[pl.ds(c * per_group, per_group)] = mixed.astype(jnp.bfloat16).reshape(
                 per_group, local, HEAD_DIM
             )
@@ -231,6 +249,7 @@
     busy = (lane < held).astype(jnp.int32)
     head = jnp.minimum(index // slots * held + lane, heads - 1)
     place = jnp.stack([head, busy]).astype(jnp.int32)
+    info = jnp.concatenate([place, counts, plan, group_mask.reshape(-1)])
     smem = pl.BlockSpec(memory_space=pltpu.SMEM)
     vmem = pl.BlockSpec(memory_space=pltpu.VMEM)
 
@@ -240,7 +259,7 @@
     result = pl.pallas_call(
         attention_kernel,
         out_shape=jax.ShapeDtypeStruct((n_dev, local, HEAD_DIM), jnp.bfloat16),
-        in_specs=[smem, smem, smem, smem, vmem, vmem],
+        in_specs=[smem, vmem, vmem],
         out_specs=vmem,
         scratch_shapes=[
             pltpu.VMEM((GROUPS, rows, HEAD_DIM), jnp.bfloat16),
@@ -250,7 +269,7 @@
         ],
         compiler_params=pltpu.CompilerParams(vmem_limit_bytes=40 * 1024 * 1024),
         name="attention",
-    )(counts, plan, group_mask, place, got, gate_table)
+    )(info, got, gate_table)
     back = lax.all_to_all(result, axes, split_axis=0, concat_axis=0, tiled=True)
     return pl.pallas_call(
         functools.partial(unpack_kernel, parts, held),

time: 75.5 us -> 73.3 us (0.971)
  Pallas kernels: 11.7 us -> 8.83 us
    pallas_call x1, Pallas kernels: 8.44 us -> 5.77 us  [head_each(): pl.pallas_call(attention_kernel, out_shape=jax.ShapeDtypeStruct((n_dev, l...]
where the time goes in v1:
time: 73.3 us; the launch traced here: 72.7 us
  waiting for transfers between devices  36.7 us (50%)
  blocking collectives  19.9 us (27%)
  Pallas kernels  8.83 us (12%)
  starting transfers between devices  7.1 us (10%)
    all_to_all x1, waiting for transfers between devices, head_each(): got = lax.all_to_all(sent, axes, split_axis=0, concat_axis=0, tiled=True)  36.7 us
    all_to_all x1, blocking collectives, head_each(): back = lax.all_to_all(result, axes, split_axis=0, concat_axis=0, tiled=True)  19.9 us
    all_to_all x1, starting transfers between devices, head_each(): got = lax.all_to_all(sent, axes, split_axis=0, concat_axis=0, tiled=True)  7.1 us
    pallas_call x1, Pallas kernels, head_each(): pl.pallas_call(attention_kernel, out_shape=jax.ShapeDtypeStruct((n_dev, l...  5.77 us
    pallas_call x1, Pallas kernels, pack(): pl.pallas_call(functools.partial(pack_kernel, parts, held), out_shape=jax...  2.32 us
  transfers between devices with their start and end apart: 1, of which 1 were waited for; matrix products, arithmetic and copies ran while one was open for 0% of the time, Pallas kernels for 0%

profile of v1, /device:TPU:1, one launch (start us, length us, event | category | flops | bytes accessed | tf_op | source)
XLA Modules:
  0.0 72.7 jit_solution(13674563323047853604)
XLA Ops:
  0.0 2.3 %pack.1 = bf16[32,3,64,128]{3,2,1,0:T(8,128)(2,1)} custom-call(bf16[64,3072]{1,0:T(8,128)(2,1)} %q_ref.1, bf16[64,3072]{1,0:T(8,128)(2,1)} %k_ref.1, bf16[64,3072]{1,0:T(8,128)(2,1)} %v_ref.1), custom_call_target="tpu_custom_call" | custom-call | tf_op jit(solution)/shard_map/pack/pallas_call | solution.py:126
  2.3 0.0 copy-start.1
  2.3 0.0 copy-start.2
  2.4 0.0 copy-start.3
  2.4 0.0 copy-start
  2.4 7.1 %all-to-all-start = ((bf16[32,3,64,128]{3,2,1,0:T(8,128)(2,1)}), bf16[32,3,64,128]{3,2,1,0:T(8,128)(2,1)S(1)}, u32[]{:S(2)}, u32[]{:S(2)}) async-start(bf16[32,3,64,128]{3,2,1,0:T(8,128)(2,1)} %pack.1), calls=%async_computation | async-start | bytes 3145728 | tf_op jit(solution)/shard_map/all_to_all | solution.py:257
  9.5 0.0 copy-done.1
  9.5 0.1 reshape.3
  9.6 0.0 copy-done.2
  9.6 0.0 copy-done.3
  9.6 0.1 concatenate.3.info_ref
  9.7 36.7 %all-to-all-done.got_ref = bf16[32,3,64,128]{3,2,1,0:T(8,128)(2,1)S(1)} async-done(((bf16[32,3,64,128]{3,2,1,0:T(8,128)(2,1)}), bf16[32,3,64,128]{3,2,1,0:T(8,128)(2,1)S(1)}, u32[]{:S(2)}, u32[]{:S(2)}) %all-to-all-start) | async-done | bytes 1572896 | tf_op jit(solution)/shard_map/all_to_all | solution.py:257
  46.4 0.0 copy-done
  46.4 5.8 %attention.1 = bf16[32,64,128]{2,1,0:T(8,128)(2,1)S(1)} custom-call(s32[26]{0:T(128)S(1)} %concatenate.3.info_ref, bf16[32,3,64,128]{3,2,1,0:T(8,128)(2,1)S(1)} %all-to-all-done.got_ref, f32[8,3072]{1,0:T(8,128)S(1)} %copy-done), custom_call_target="tpu_custom_call" | custom-call | tf_op jit(solution)/shard_map/attention/pallas_call | solution.py:259
  52.1 19.9 %all_to_all.10.in_ref = bf16[32,64,128]{2,1,0:T(8,128)(2,1)S(1)} all-to-all(bf16[32,64,128]{2,1,0:T(8,128)(2,1)S(1)} %attention.1), channel_id=1, replica_groups=mesh['seq'=16,'head'=2] {'seq','head'}, dimensions={0} | all-to-all | bytes 1048576 | tf_op jit(solution)/shard_map/all_to_all | solution.py:273
  72.0 0.7 %unpack.1 = bf16[64,3072]{1,0:T(8,128)(2,1)} custom-call(bf16[32,64,128]{2,1,0:T(8,128)(2,1)S(1)} %all_to_all.10.in_ref), custom_call_target="tpu_custom_call" | custom-call | tf_op jit(solution)/shard_map/unpack/pallas_call | solution.py:274
Async XLA Ops:
  2.3 7.2 %copy-start.1 = (s32[4,4]{1,0:T(4,128)S(1)}, s32[4,4]{1,0:T(4,128)}, u32[]{:S(2)}) copy-start(s32[4,4]{1,0:T(4,128)} %param.12) | copy-start | bytes 196
  2.3 7.3 %copy-start.2 = (s32[4]{0:T(128)S(1)}, s32[4]{0:T(128)}, u32[]{:S(2)}) copy-start(s32[4]{0:T(128)} %param.10) | copy-start | bytes 52
  2.4 7.3 %copy-start.3 = (s32[4]{0:T(128)S(1)}, s32[4]{0:T(128)}, u32[]{:S(2)}) copy-start(s32[4]{0:T(128)} %param.11) | copy-start | bytes 52
  2.4 44.0 %copy-start = (f32[8,3072]{1,0:T(8,128)S(1)}, f32[8,3072]{1,0:T(8,128)}, u32[]{:S(2)}) copy-start(f32[8,3072]{1,0:T(8,128)} %gate_ref.1) | copy-start | bytes 294916
  2.4 44.0 %all-to-all-start = ((bf16[32,3,64,128]{3,2,1,0:T(8,128)(2,1)}), bf16[32,3,64,128]{3,2,1,0:T(8,128)(2,1)S(1)}, u32[]{:S(2)}, u32[]{:S(2)}) async-start(bf16[32,3,64,128]{3,2,1,0:T(8,128)(2,1)} %pack.1), calls=%async_computation | async-start | bytes 3145728 | tf_op jit(solution)/shard_map/all_to_all | solution.py:257

commit v2 on v1

--- a/solution.py
+++ b/solution.py
@@ -151,12 +151,13 @@
 
 
 def attention_kernel(
-    info_ref, got_ref, gate_ref, out_ref, bias_ref, score_ref, top_ref, mixed_ref
+    info_ref, got_ref, gate_ref, out_ref, bias_ref, score_ref, mixed_ref, *pair_refs
 ):
     n_dev, _, local, _ = got_ref.shape
     per_group = n_dev // GROUPS
     rows = per_group * local
     factor = 1.0 / math.sqrt(HEAD_DIM)
+    own_refs, top_refs = pair_refs[:2], pair_refs[2:]
     head = info_ref[0]
     busy = info_ref[1]
 
@@ -200,10 +201,16 @@
                 weights, jnp.concatenate([part(d, 2), ones], axis=1), preferred_element_type=jnp.float32
             )
 
-        @pl.loop(0, GROUPS)
-        def _(c):
+        def own_scores(c):
+            scores = score(c, c)
+            own_refs[c % 2][...] = scores
+            top_refs[c % 2][...] = lane_top(scores, jnp.float32(-1e30))
+
+        for c in range(GROUPS):
             bias_ref[c] = jnp.where(place < count_of(c), 0.0, -1e30).astype(jnp.bfloat16)
-            top_ref[...] = jnp.full(top_ref.shape, -1e30, jnp.float32)
+        own_scores(0)
+        for c in range(GROUPS):
+            top_ref = top_refs[c % 2]
 
             @pl.loop(0, c)
             def _(d):
@@ -213,11 +220,12 @@
                     score_ref[d] = scores
                     top_ref[...] = lane_top(scores, top_ref[...])
 
-            own = score(c, c)
-            top = jnp.max(lane_top(own, top_ref[...]), axis=1, keepdims=True) * factor
+            top = jnp.max(top_ref[...], axis=1, keepdims=True) * factor
             top = jnp.broadcast_to(top, top_ref.shape)
             top_ref[...] = top
-            mixed_ref[...] = product(own, top, c)
+            if c + 1 < GROUPS:
+                own_scores(c + 1)
+            mixed_ref[...] = product(own_refs[c % 2][...], top, c)
 
             @pl.loop(0, c)
             def _(d):
@@ -228,7 +236,7 @@
             gate = jnp.sum(jnp.where(level == level_of(c), gates, jnp.float32(0.0)), axis=0, keepdims=True)
             mixed = mixed_ref[:, :HEAD_DIM] / mixed_ref[:, HEAD_DIM:] * gate
             mixed = jnp.where(place < count_of(c), mixed, jnp.float32(0.0))
-            out_ref[pl.ds(c * per_group, per_group)] = mixed.astype(jnp.bfloat16).reshape(
+            out_ref[c * per_group : (c + 1) * per_group] = mixed.astype(jnp.bfloat16).reshape(
                 per_group, local, HEAD_DIM
             )
 
@@ -264,8 +272,11 @@
         scratch_shapes=[
             pltpu.VMEM((GROUPS, rows, HEAD_DIM), jnp.bfloat16),
             pltpu.VMEM((GROUPS - 1, rows, rows), jnp.float32),
+            pltpu.VMEM((rows, 2 * HEAD_DIM), jnp.float32),
+            pltpu.VMEM((rows, rows), jnp.float32),
+            pltpu.VMEM((rows, rows), jnp.float32),
             pltpu.VMEM((rows, HEAD_DIM), jnp.float32),
-            pltpu.VMEM((rows, 2 * HEAD_DIM), jnp.float32),
+            pltpu.VMEM((rows, HEAD_DIM), jnp.float32),
         ],
         compiler_params=pltpu.CompilerParams(vmem_limit_bytes=40 * 1024 * 1024),
         name="attention",

time: 73.3 us -> 71.7 us (0.978)
  Pallas kernels: 8.83 us -> 6.86 us
    pallas_call x1, Pallas kernels: 5.77 us -> 3.8 us  [head_each(): pl.pallas_call(attention_kernel, out_shape=jax.ShapeDtypeStruct((n_dev, l...]
where the time goes in v2:
time: 71.7 us; the launch traced here: 70.8 us
  waiting for transfers between devices  36.7 us (51%)
  blocking collectives  19.9 us (28%)
  starting transfers between devices  7.1 us (10%)
  Pallas kernels  6.86 us (10%)
    all_to_all x1, waiting for transfers between devices, head_each(): got = lax.all_to_all(sent, axes, split_axis=0, concat_axis=0, tiled=True)  36.7 us
    all_to_all x1, blocking collectives, head_each(): back = lax.all_to_all(result, axes, split_axis=0, concat_axis=0, tiled=True)  19.9 us
    all_to_all x1, starting transfers between devices, head_each(): got = lax.all_to_all(sent, axes, split_axis=0, concat_axis=0, tiled=True)  7.1 us
    pallas_call x1, Pallas kernels, head_each(): pl.pallas_call(attention_kernel, out_shape=jax.ShapeDtypeStruct((n_dev, l...  3.8 us
    pallas_call x1, Pallas kernels, pack(): pl.pallas_call(functools.partial(pack_kernel, parts, held), out_shape=jax...  2.32 us
  transfers between devices with their start and end apart: 1, of which 1 were waited for; matrix products, arithmetic and copies ran while one was open for 0% of the time, Pallas kernels for 0%

profile of v2, /device:TPU:1, one launch (start us, length us, event | category | flops | bytes accessed | tf_op | source)
XLA Modules:
  0.0 70.8 jit_solution(9636525270812175844)
XLA Ops:
  0.0 2.3 %pack.1 = bf16[32,3,64,128]{3,2,1,0:T(8,128)(2,1)} custom-call(bf16[64,3072]{1,0:T(8,128)(2,1)} %q_ref.1, bf16[64,3072]{1,0:T(8,128)(2,1)} %k_ref.1, bf16[64,3072]{1,0:T(8,128)(2,1)} %v_ref.1), custom_call_target="tpu_custom_call" | custom-call | tf_op jit(solution)/shard_map/pack/pallas_call | solution.py:126
  2.3 0.0 copy-start.1
  2.3 0.0 copy-start.2
  2.4 0.0 copy-start.3
  2.4 0.0 copy-start
  2.4 7.1 %all-to-all-start = ((bf16[32,3,64,128]{3,2,1,0:T(8,128)(2,1)}), bf16[32,3,64,128]{3,2,1,0:T(8,128)(2,1)S(1)}, u32[]{:S(2)}, u32[]{:S(2)}) async-start(bf16[32,3,64,128]{3,2,1,0:T(8,128)(2,1)} %pack.1), calls=%async_computation | async-start | bytes 3145728 | tf_op jit(solution)/shard_map/all_to_all | solution.py:265
  9.5 0.0 copy-done.1
  9.5 0.1 reshape.3
  9.6 0.0 copy-done.2
  9.6 0.0 copy-done.3
  9.6 0.1 concatenate.3.info_ref
  9.7 36.7 %all-to-all-done.got_ref = bf16[32,3,64,128]{3,2,1,0:T(8,128)(2,1)S(1)} async-done(((bf16[32,3,64,128]{3,2,1,0:T(8,128)(2,1)}), bf16[32,3,64,128]{3,2,1,0:T(8,128)(2,1)S(1)}, u32[]{:S(2)}, u32[]{:S(2)}) %all-to-all-start) | async-done | bytes 1572896 | tf_op jit(solution)/shard_map/all_to_all | solution.py:265
  46.4 0.0 copy-done
  46.4 3.8 %attention.1 = bf16[32,64,128]{2,1,0:T(8,128)(2,1)S(1)} custom-call(s32[26]{0:T(128)S(1)} %concatenate.3.info_ref, bf16[32,3,64,128]{3,2,1,0:T(8,128)(2,1)S(1)} %all-to-all-done.got_ref, f32[8,3072]{1,0:T(8,128)S(1)} %copy-done), custom_call_target="tpu_custom_call" | custom-call | tf_op jit(solution)/shard_map/attention/pallas_call | solution.py:267
  50.2 19.9 %all_to_all.10.in_ref = bf16[32,64,128]{2,1,0:T(8,128)(2,1)S(1)} all-to-all(bf16[32,64,128]{2,1,0:T(8,128)(2,1)S(1)} %attention.1), channel_id=1, replica_groups=mesh['seq'=16,'head'=2] {'seq','head'}, dimensions={0} | all-to-all | bytes 1048576 | tf_op jit(solution)/shard_map/all_to_all | solution.py:284
  70.0 0.7 %unpack.1 = bf16[64,3072]{1,0:T(8,128)(2,1)} custom-call(bf16[32,64,128]{2,1,0:T(8,128)(2,1)S(1)} %all_to_all.10.in_ref), custom_call_target="tpu_custom_call" | custom-call | tf_op jit(solution)/shard_map/unpack/pallas_call | solution.py:285
Async XLA Ops:
  2.3 7.2 %copy-start.1 = (s32[4,4]{1,0:T(4,128)S(1)}, s32[4,4]{1,0:T(4,128)}, u32[]{:S(2)}) copy-start(s32[4,4]{1,0:T(4,128)} %param.12) | copy-start | bytes 196
  2.3 7.3 %copy-start.2 = (s32[4]{0:T(128)S(1)}, s32[4]{0:T(128)}, u32[]{:S(2)}) copy-start(s32[4]{0:T(128)} %param.10) | copy-start | bytes 52
  2.4 7.3 %copy-start.3 = (s32[4]{0:T(128)S(1)}, s32[4]{0:T(128)}, u32[]{:S(2)}) copy-start(s32[4]{0:T(128)} %param.11) | copy-start | bytes 52
  2.4 44.0 %copy-start = (f32[8,3072]{1,0:T(8,128)S(1)}, f32[8,3072]{1,0:T(8,128)}, u32[]{:S(2)}) copy-start(f32[8,3072]{1,0:T(8,128)} %gate_ref.1) | copy-start | bytes 294916
  2.4 44.0 %all-to-all-start = ((bf16[32,3,64,128]{3,2,1,0:T(8,128)(2,1)}), bf16[32,3,64,128]{3,2,1,0:T(8,128)(2,1)S(1)}, u32[]{:S(2)}, u32[]{:S(2)}) async-start(bf16[32,3,64,128]{3,2,1,0:T(8,128)(2,1)} %pack.1), calls=%async_computation | async-start | bytes 3145728 | tf_op jit(solution)/shard_map/all_to_all | solution.py:265

commit v3 on v2

--- a/solution.py
+++ b/solution.py
@@ -151,7 +151,7 @@
 
 
 def attention_kernel(
-    info_ref, got_ref, gate_ref, out_ref, bias_ref, score_ref, mixed_ref, *pair_refs
+    info_ref, got_ref, gate_ref, out_ref, bias_ref, score_ref, mixed_ref, sum_ref, *pair_refs
 ):
     n_dev, _, local, _ = got_ref.shape
     per_group = n_dev // GROUPS
@@ -177,7 +177,6 @@
         place = lax.broadcasted_iota(jnp.int32, (rows, HEAD_DIM), 0)
         lane = lax.broadcasted_iota(jnp.int32, (rows, HEAD_DIM), 1)
         one = jnp.where(lane == 0, 1.0, 0.0).astype(jnp.bfloat16)
-        ones = jnp.ones((rows, HEAD_DIM), jnp.bfloat16)
 
         def part(group, kind):
             return got_ref[pl.ds(group * per_group, per_group), kind].reshape(rows, HEAD_DIM)
@@ -196,9 +195,10 @@
 
         def product(scores, top, d):
             shift = jnp.concatenate([top] * (rows // HEAD_DIM), axis=1)
-            weights = jnp.exp(scores * factor - shift).astype(jnp.bfloat16)
-            return jnp.dot(
-                weights, jnp.concatenate([part(d, 2), ones], axis=1), preferred_element_type=jnp.float32
+            weights = jnp.exp(scores * factor - shift)
+            pieces = [weights[:, i : i + HEAD_DIM] for i in range(0, rows, HEAD_DIM)]
+            return functools.reduce(jnp.add, pieces), jnp.dot(
+                weights.astype(jnp.bfloat16), part(d, 2), preferred_element_type=jnp.float32
             )
 
         def own_scores(c):
@@ -225,16 +225,19 @@
             top_ref[...] = top
             if c + 1 < GROUPS:
                 own_scores(c + 1)
-            mixed_ref[...] = product(own_refs[c % 2][...], top, c)
+            sum_ref[...], mixed_ref[...] = product(own_refs[c % 2][...], top, c)
 
             @pl.loop(0, c)
             def _(d):
                 @pl.when(sees(c, d))
                 def _():
-                    mixed_ref[...] += product(score_ref[d], top_ref[...], d)
+                    sums, mixed = product(score_ref[d], top_ref[...], d)
+                    sum_ref[...] += sums
+                    mixed_ref[...] += mixed
 
             gate = jnp.sum(jnp.where(level == level_of(c), gates, jnp.float32(0.0)), axis=0, keepdims=True)
-            mixed = mixed_ref[:, :HEAD_DIM] / mixed_ref[:, HEAD_DIM:] * gate
+            total = jnp.sum(sum_ref[...], axis=1, keepdims=True)
+            mixed = mixed_ref[...] / total * gate
             mixed = jnp.where(place < count_of(c), mixed, jnp.float32(0.0))
             out_ref[c * per_group : (c + 1) * per_group] = mixed.astype(jnp.bfloat16).reshape(
                 per_group, local, HEAD_DIM
@@ -272,7 +275,8 @@
         scratch_shapes=[
             pltpu.VMEM((GROUPS, rows, HEAD_DIM), jnp.bfloat16),
             pltpu.VMEM((GROUPS - 1, rows, rows), jnp.float32),
-            pltpu.VMEM((rows, 2 * HEAD_DIM), jnp.float32),
+            pltpu.VMEM((rows, HEAD_DIM), jnp.float32),
+            pltpu.VMEM((rows, HEAD_DIM), jnp.float32),
             pltpu.VMEM((rows, rows), jnp.float32),
             pltpu.VMEM((rows, rows), jnp.float32),
             pltpu.VMEM((rows, HEAD_DIM), jnp.float32),

time: 71.7 us -> 71.3 us (level); the launches traced: 70.8 us -> 71.8 us
  Pallas kernels: 6.86 us -> 7.85 us
    pallas_call x1, Pallas kernels: 3.8 us -> 4.79 us  [head_each(): pl.pallas_call(attention_kernel, out_shape=jax.ShapeDtypeStruct((n_dev, l...]
where the time goes in v3:
time: 71.3 us; the launch traced here: 71.8 us
  waiting for transfers between devices  36.7 us (51%)
  blocking collectives  19.9 us (28%)
  Pallas kernels  7.85 us (11%)
  starting transfers between devices  7.1 us (10%)
    all_to_all x1, waiting for transfers between devices, head_each(): got = lax.all_to_all(sent, axes, split_axis=0, concat_axis=0, tiled=True)  36.7 us
    all_to_all x1, blocking collectives, head_each(): back = lax.all_to_all(result, axes, split_axis=0, concat_axis=0, tiled=True)  19.9 us
    all_to_all x1, starting transfers between devices, head_each(): got = lax.all_to_all(sent, axes, split_axis=0, concat_axis=0, tiled=True)  7.1 us
    pallas_call x1, Pallas kernels, head_each(): pl.pallas_call(attention_kernel, out_shape=jax.ShapeDtypeStruct((n_dev, l...  4.79 us
    pallas_call x1, Pallas kernels, pack(): pl.pallas_call(functools.partial(pack_kernel, parts, held), out_shape=jax...  2.32 us
  transfers between devices with their start and end apart: 1, of which 1 were waited for; matrix products, arithmetic and copies ran while one was open for 0% of the time, Pallas kernels for 0%

profile of v3, /device:TPU:1, one launch (start us, length us, event | category | flops | bytes accessed | tf_op | source)
XLA Modules:
  0.0 71.8 jit_solution(10368920103899286503)
XLA Ops:
  0.0 2.3 %pack.1 = bf16[32,3,64,128]{3,2,1,0:T(8,128)(2,1)} custom-call(bf16[64,3072]{1,0:T(8,128)(2,1)} %q_ref.1, bf16[64,3072]{1,0:T(8,128)(2,1)} %k_ref.1, bf16[64,3072]{1,0:T(8,128)(2,1)} %v_ref.1), custom_call_target="tpu_custom_call" | custom-call | tf_op jit(solution)/shard_map/pack/pallas_call | solution.py:126
  2.3 0.0 copy-start.1
  2.3 0.0 copy-start.2
  2.4 0.0 copy-start.3
  2.4 0.0 copy-start
  2.4 7.1 %all-to-all-start = ((bf16[32,3,64,128]{3,2,1,0:T(8,128)(2,1)}), bf16[32,3,64,128]{3,2,1,0:T(8,128)(2,1)S(1)}, u32[]{:S(2)}, u32[]{:S(2)}) async-start(bf16[32,3,64,128]{3,2,1,0:T(8,128)(2,1)} %pack.1), calls=%async_computation | async-start | bytes 3145728 | tf_op jit(solution)/shard_map/all_to_all | solution.py:268
  9.5 0.0 copy-done.1
  9.5 0.1 reshape.3
  9.6 0.0 copy-done.2
  9.6 0.0 copy-done.3
  9.6 0.1 concatenate.3.info_ref
  9.7 36.7 %all-to-all-done.got_ref = bf16[32,3,64,128]{3,2,1,0:T(8,128)(2,1)S(1)} async-done(((bf16[32,3,64,128]{3,2,1,0:T(8,128)(2,1)}), bf16[32,3,64,128]{3,2,1,0:T(8,128)(2,1)S(1)}, u32[]{:S(2)}, u32[]{:S(2)}) %all-to-all-start) | async-done | bytes 1572896 | tf_op jit(solution)/shard_map/all_to_all | solution.py:268
  46.4 0.0 copy-done
  46.4 4.8 %attention.1 = bf16[32,64,128]{2,1,0:T(8,128)(2,1)S(1)} custom-call(s32[26]{0:T(128)S(1)} %concatenate.3.info_ref, bf16[32,3,64,128]{3,2,1,0:T(8,128)(2,1)S(1)} %all-to-all-done.got_ref, f32[8,3072]{1,0:T(8,128)S(1)} %copy-done), custom_call_target="tpu_custom_call" | custom-call | tf_op jit(solution)/shard_map/attention/pallas_call | solution.py:270
  51.2 19.9 %all_to_all.10.in_ref = bf16[32,64,128]{2,1,0:T(8,128)(2,1)S(1)} all-to-all(bf16[32,64,128]{2,1,0:T(8,128)(2,1)S(1)} %attention.1), channel_id=1, replica_groups=mesh['seq'=16,'head'=2] {'seq','head'}, dimensions={0} | all-to-all | bytes 1048576 | tf_op jit(solution)/shard_map/all_to_all | solution.py:288
  71.0 0.7 %unpack.1 = bf16[64,3072]{1,0:T(8,128)(2,1)} custom-call(bf16[32,64,128]{2,1,0:T(8,128)(2,1)S(1)} %all_to_all.10.in_ref), custom_call_target="tpu_custom_call" | custom-call | tf_op jit(solution)/shard_map/unpack/pallas_call | solution.py:289
Async XLA Ops:
  2.3 7.2 %copy-start.1 = (s32[4,4]{1,0:T(4,128)S(1)}, s32[4,4]{1,0:T(4,128)}, u32[]{:S(2)}) copy-start(s32[4,4]{1,0:T(4,128)} %param.12) | copy-start | bytes 196
  2.3 7.3 %copy-start.2 = (s32[4]{0:T(128)S(1)}, s32[4]{0:T(128)}, u32[]{:S(2)}) copy-start(s32[4]{0:T(128)} %param.10) | copy-start | bytes 52
  2.4 7.3 %copy-start.3 = (s32[4]{0:T(128)S(1)}, s32[4]{0:T(128)}, u32[]{:S(2)}) copy-start(s32[4]{0:T(128)} %param.11) | copy-start | bytes 52
  2.4 44.0 %copy-start = (f32[8,3072]{1,0:T(8,128)S(1)}, f32[8,3072]{1,0:T(8,128)}, u32[]{:S(2)}) copy-start(f32[8,3072]{1,0:T(8,128)} %gate_ref.1) | copy-start | bytes 294916
  2.4 44.0 %all-to-all-start = ((bf16[32,3,64,128]{3,2,1,0:T(8,128)(2,1)}), bf16[32,3,64,128]{3,2,1,0:T(8,128)(2,1)S(1)}, u32[]{:S(2)}, u32[]{:S(2)}) async-start(bf16[32,3,64,128]{3,2,1,0:T(8,128)(2,1)} %pack.1), calls=%async_computation | async-start | bytes 3145728 | tf_op jit(solution)/shard_map/all_to_all | solution.py:268

commit v4 on v3

--- a/solution.py
+++ b/solution.py
@@ -151,7 +151,7 @@
 
 
 def attention_kernel(
-    info_ref, got_ref, gate_ref, out_ref, bias_ref, score_ref, mixed_ref, sum_ref, *pair_refs
+    info_ref, got_ref, gate_ref, out_ref, score_ref, mixed_ref, sum_ref, *pair_refs
 ):
     n_dev, _, local, _ = got_ref.shape
     per_group = n_dev // GROUPS
@@ -175,19 +175,17 @@
         gates = gate_ref[:, pl.ds(pl.multiple_of(head * HEAD_DIM, HEAD_DIM), HEAD_DIM)]
         level = lax.broadcasted_iota(jnp.int32, (LEVELS, HEAD_DIM), 0)
         place = lax.broadcasted_iota(jnp.int32, (rows, HEAD_DIM), 0)
-        lane = lax.broadcasted_iota(jnp.int32, (rows, HEAD_DIM), 1)
-        one = jnp.where(lane == 0, 1.0, 0.0).astype(jnp.bfloat16)
+        column = rows // 2 + lax.broadcasted_iota(jnp.int32, (1, rows // 2), 1)
 
         def part(group, kind):
             return got_ref[pl.ds(group * per_group, per_group), kind].reshape(rows, HEAD_DIM)
 
         def score(c, d):
-            return lax.dot_general(
-                jnp.concatenate([part(c, 0), one], axis=1),
-                jnp.concatenate([part(d, 1), bias_ref[d]], axis=1),
-                (((1,), (1,)), ((), ())),
-                preferred_element_type=jnp.float32,
+            scores = lax.dot_general(
+                part(c, 0), part(d, 1), (((1,), (1,)), ((), ())), preferred_element_type=jnp.float32
             )
+            late = jnp.where(column < count_of(d), scores[:, rows // 2 :], jnp.float32(-1e30))
+            return jnp.concatenate([scores[:, : rows // 2], late], axis=1)
 
         def lane_top(scores, top):
             pieces = [scores[:, i : i + HEAD_DIM] for i in range(0, rows, HEAD_DIM)]
@@ -206,8 +204,6 @@
             own_refs[c % 2][...] = scores
             top_refs[c % 2][...] = lane_top(scores, jnp.float32(-1e30))
 
-        for c in range(GROUPS):
-            bias_ref[c] = jnp.where(place < count_of(c), 0.0, -1e30).astype(jnp.bfloat16)
         own_scores(0)
         for c in range(GROUPS):
             top_ref = top_refs[c % 2]
@@ -273,7 +269,6 @@
         in_specs=[smem, vmem, vmem],
         out_specs=vmem,
         scratch_shapes=[
-            pltpu.VMEM((GROUPS, rows, HEAD_DIM), jnp.bfloat16),
             pltpu.VMEM((GROUPS - 1, rows, rows), jnp.float32),
             pltpu.VMEM((rows, HEAD_DIM), jnp.float32),
             pltpu.VMEM((rows, HEAD_DIM), jnp.float32),

time: 71.3 us -> 72.8 us (1.021)
  Pallas kernels: 7.85 us -> 9.6 us
    pallas_call x1, Pallas kernels: 4.79 us -> 6.54 us  [head_each(): pl.pallas_call(attention_kernel, out_shape=jax.ShapeDtypeStruct((n_dev, l...]
where the time goes in v4:
time: 72.8 us; the launch traced here: 73.5 us
  waiting for transfers between devices  36.7 us (50%)
  blocking collectives  19.9 us (27%)
  Pallas kernels  9.6 us (13%)
  starting transfers between devices  7.1 us (10%)
    all_to_all x1, waiting for transfers between devices, head_each(): got = lax.all_to_all(sent, axes, split_axis=0, concat_axis=0, tiled=True)  36.7 us
    all_to_all x1, blocking collectives, head_each(): back = lax.all_to_all(result, axes, split_axis=0, concat_axis=0, tiled=True)  19.9 us
    all_to_all x1, starting transfers between devices, head_each(): got = lax.all_to_all(sent, axes, split_axis=0, concat_axis=0, tiled=True)  7.1 us
    pallas_call x1, Pallas kernels, head_each(): pl.pallas_call(attention_kernel, out_shape=jax.ShapeDtypeStruct((n_dev, l...  6.54 us
    pallas_call x1, Pallas kernels, pack(): pl.pallas_call(functools.partial(pack_kernel, parts, held), out_shape=jax...  2.32 us
  transfers between devices with their start and end apart: 1, of which 1 were waited for; matrix products, arithmetic and copies ran while one was open for 0% of the time, Pallas kernels for 0%

profile of v4, /device:TPU:1, one launch (start us, length us, event | category | flops | bytes accessed | tf_op | source)
XLA Modules:
  0.0 73.5 jit_solution(8622407793713728935)
XLA Ops:
  0.0 2.3 %pack.1 = bf16[32,3,64,128]{3,2,1,0:T(8,128)(2,1)} custom-call(bf16[64,3072]{1,0:T(8,128)(2,1)} %q_ref.1, bf16[64,3072]{1,0:T(8,128)(2,1)} %k_ref.1, bf16[64,3072]{1,0:T(8,128)(2,1)} %v_ref.1), custom_call_target="tpu_custom_call" | custom-call | tf_op jit(solution)/shard_map/pack/pallas_call | solution.py:126
  2.3 0.0 copy-start.1
  2.3 0.0 copy-start.2
  2.4 0.0 copy-start.3
  2.4 0.0 copy-start
  2.4 7.1 %all-to-all-start = ((bf16[32,3,64,128]{3,2,1,0:T(8,128)(2,1)}), bf16[32,3,64,128]{3,2,1,0:T(8,128)(2,1)S(1)}, u32[]{:S(2)}, u32[]{:S(2)}) async-start(bf16[32,3,64,128]{3,2,1,0:T(8,128)(2,1)} %pack.1), calls=%async_computation | async-start | bytes 3145728 | tf_op jit(solution)/shard_map/all_to_all | solution.py:264
  9.5 0.0 copy-done.1
  9.5 0.1 reshape.3
  9.6 0.0 copy-done.2
  9.6 0.0 copy-done.3
  9.6 0.1 concatenate.3.info_ref
  9.7 36.7 %all-to-all-done.got_ref = bf16[32,3,64,128]{3,2,1,0:T(8,128)(2,1)S(1)} async-done(((bf16[32,3,64,128]{3,2,1,0:T(8,128)(2,1)}), bf16[32,3,64,128]{3,2,1,0:T(8,128)(2,1)S(1)}, u32[]{:S(2)}, u32[]{:S(2)}) %all-to-all-start) | async-done | bytes 1572896 | tf_op jit(solution)/shard_map/all_to_all | solution.py:264
  46.4 0.0 copy-done
  46.4 6.5 %attention.1 = bf16[32,64,128]{2,1,0:T(8,128)(2,1)S(1)} custom-call(s32[26]{0:T(128)S(1)} %concatenate.3.info_ref, bf16[32,3,64,128]{3,2,1,0:T(8,128)(2,1)S(1)} %all-to-all-done.got_ref, f32[8,3072]{1,0:T(8,128)S(1)} %copy-done), custom_call_target="tpu_custom_call" | custom-call | tf_op jit(solution)/shard_map/attention/pallas_call | solution.py:266
  52.9 19.9 %all_to_all.10.in_ref = bf16[32,64,128]{2,1,0:T(8,128)(2,1)S(1)} all-to-all(bf16[32,64,128]{2,1,0:T(8,128)(2,1)S(1)} %attention.1), channel_id=1, replica_groups=mesh['seq'=16,'head'=2] {'seq','head'}, dimensions={0} | all-to-all | bytes 1048576 | tf_op jit(solution)/shard_map/all_to_all | solution.py:283
  72.8 0.7 unpack.1
Async XLA Ops:
  2.3 7.2 %copy-start.1 = (s32[4,4]{1,0:T(4,128)S(1)}, s32[4,4]{1,0:T(4,128)}, u32[]{:S(2)}) copy-start(s32[4,4]{1,0:T(4,128)} %param.12) | copy-start | bytes 196
  2.3 7.3 %copy-start.2 = (s32[4]{0:T(128)S(1)}, s32[4]{0:T(128)}, u32[]{:S(2)}) copy-start(s32[4]{0:T(128)} %param.10) | copy-start | bytes 52
  2.4 7.3 %copy-start.3 = (s32[4]{0:T(128)S(1)}, s32[4]{0:T(128)}, u32[]{:S(2)}) copy-start(s32[4]{0:T(128)} %param.11) | copy-start | bytes 52
  2.4 44.0 %copy-start = (f32[8,3072]{1,0:T(8,128)S(1)}, f32[8,3072]{1,0:T(8,128)}, u32[]{:S(2)}) copy-start(f32[8,3072]{1,0:T(8,128)} %gate_ref.1) | copy-start | bytes 294916
  2.4 44.0 %all-to-all-start = ((bf16[32,3,64,128]{3,2,1,0:T(8,128)(2,1)}), bf16[32,3,64,128]{3,2,1,0:T(8,128)(2,1)S(1)}, u32[]{:S(2)}, u32[]{:S(2)}) async-start(bf16[32,3,64,128]{3,2,1,0:T(8,128)(2,1)} %pack.1), calls=%async_computation | async-start | bytes 3145728 | tf_op jit(solution)/shard_map/all_to_all | solution.py:264

commit v5 on v4

--- a/solution.py
+++ b/solution.py
@@ -156,7 +156,7 @@
     n_dev, _, local, _ = got_ref.shape
     per_group = n_dev // GROUPS
     rows = per_group * local
-    factor = 1.0 / math.sqrt(HEAD_DIM)
+    factor = math.log2(math.e) / math.sqrt(HEAD_DIM)
     own_refs, top_refs = pair_refs[:2], pair_refs[2:]
     head = info_ref[0]
     busy = info_ref[1]
@@ -193,7 +193,7 @@
 
         def product(scores, top, d):
             shift = jnp.concatenate([top] * (rows // HEAD_DIM), axis=1)
-            weights = jnp.exp(scores * factor - shift)
+            weights = jnp.exp2(scores * factor - shift)
             pieces = [weights[:, i : i + HEAD_DIM] for i in range(0, rows, HEAD_DIM)]
             return functools.reduce(jnp.add, pieces), jnp.dot(
                 weights.astype(jnp.bfloat16), part(d, 2), preferred_element_type=jnp.float32

time: 72.8 us -> 72.4 us (level); the launches traced: 73.5 us -> 71.5 us
  Pallas kernels: 9.6 us -> 7.61 us
    pallas_call x1, Pallas kernels: 6.54 us -> 4.55 us  [head_each(): pl.pallas_call(attention_kernel, out_shape=jax.ShapeDtypeStruct((n_dev, l...]
where the time goes in v5:
time: 72.4 us; the launch traced here: 71.5 us
  waiting for transfers between devices  36.7 us (51%)
  blocking collectives  19.9 us (27%)
  Pallas kernels  7.61 us (11%)
  starting transfers between devices  7.1 us (10%)
    all_to_all x1, waiting for transfers between devices, head_each(): got = lax.all_to_all(sent, axes, split_axis=0, concat_axis=0, tiled=True)  36.7 us
    all_to_all x1, blocking collectives, head_each(): back = lax.all_to_all(result, axes, split_axis=0, concat_axis=0, tiled=True)  19.9 us
    all_to_all x1, starting transfers between devices, head_each(): got = lax.all_to_all(sent, axes, split_axis=0, concat_axis=0, tiled=True)  7.1 us
    pallas_call x1, Pallas kernels, head_each(): pl.pallas_call(attention_kernel, out_shape=jax.ShapeDtypeStruct((n_dev, l...  4.55 us
    pallas_call x1, Pallas kernels, pack(): pl.pallas_call(functools.partial(pack_kernel, parts, held), out_shape=jax...  2.32 us
  transfers between devices with their start and end apart: 1, of which 1 were waited for; matrix products, arithmetic and copies ran while one was open for 0% of the time, Pallas kernels for 0%

profile of v5, /device:TPU:1, one launch (start us, length us, event | category | flops | bytes accessed | tf_op | source)
XLA Modules:
  0.0 71.5 jit_solution(11986528819928089776)
XLA Ops:
  0.0 2.3 %pack.1 = bf16[32,3,64,128]{3,2,1,0:T(8,128)(2,1)} custom-call(bf16[64,3072]{1,0:T(8,128)(2,1)} %q_ref.1, bf16[64,3072]{1,0:T(8,128)(2,1)} %k_ref.1, bf16[64,3072]{1,0:T(8,128)(2,1)} %v_ref.1), custom_call_target="tpu_custom_call" | custom-call | tf_op jit(solution)/shard_map/pack/pallas_call | solution.py:126
  2.3 0.0 copy-start.1
  2.3 0.0 copy-start.2
  2.4 0.0 copy-start.3
  2.4 0.0 copy-start
  2.4 7.1 %all-to-all-start = ((bf16[32,3,64,128]{3,2,1,0:T(8,128)(2,1)}), bf16[32,3,64,128]{3,2,1,0:T(8,128)(2,1)S(1)}, u32[]{:S(2)}, u32[]{:S(2)}) async-start(bf16[32,3,64,128]{3,2,1,0:T(8,128)(2,1)} %pack.1), calls=%async_computation | async-start | bytes 3145728 | tf_op jit(solution)/shard_map/all_to_all | solution.py:264
  9.5 0.0 copy-done.1
  9.5 0.1 reshape.3
  9.6 0.0 copy-done.2
  9.6 0.0 copy-done.3
  9.6 0.1 concatenate.3.info_ref
  9.7 36.7 %all-to-all-done.got_ref = bf16[32,3,64,128]{3,2,1,0:T(8,128)(2,1)S(1)} async-done(((bf16[32,3,64,128]{3,2,1,0:T(8,128)(2,1)}), bf16[32,3,64,128]{3,2,1,0:T(8,128)(2,1)S(1)}, u32[]{:S(2)}, u32[]{:S(2)}) %all-to-all-start) | async-done | bytes 1572896 | tf_op jit(solution)/shard_map/all_to_all | solution.py:264
  46.4 0.0 copy-done
  46.4 4.5 %attention.1 = bf16[32,64,128]{2,1,0:T(8,128)(2,1)S(1)} custom-call(s32[26]{0:T(128)S(1)} %concatenate.3.info_ref, bf16[32,3,64,128]{3,2,1,0:T(8,128)(2,1)S(1)} %all-to-all-done.got_ref, f32[8,3072]{1,0:T(8,128)S(1)} %copy-done), custom_call_target="tpu_custom_call" | custom-call | tf_op jit(solution)/shard_map/attention/pallas_call | solution.py:266
  50.9 19.9 %all_to_all.10.in_ref = bf16[32,64,128]{2,1,0:T(8,128)(2,1)S(1)} all-to-all(bf16[32,64,128]{2,1,0:T(8,128)(2,1)S(1)} %attention.1), channel_id=1, replica_groups=mesh['seq'=16,'head'=2] {'seq','head'}, dimensions={0} | all-to-all | bytes 1048576 | tf_op jit(solution)/shard_map/all_to_all | solution.py:283
  70.8 0.7 %unpack.1 = bf16[64,3072]{1,0:T(8,128)(2,1)} custom-call(bf16[32,64,128]{2,1,0:T(8,128)(2,1)S(1)} %all_to_all.10.in_ref), custom_call_target="tpu_custom_call" | custom-call | tf_op jit(solution)/shard_map/unpack/pallas_call | solution.py:284
Async XLA Ops:
  2.3 7.2 %copy-start.1 = (s32[4,4]{1,0:T(4,128)S(1)}, s32[4,4]{1,0:T(4,128)}, u32[]{:S(2)}) copy-start(s32[4,4]{1,0:T(4,128)} %param.12) | copy-start | bytes 196
  2.3 7.3 %copy-start.2 = (s32[4]{0:T(128)S(1)}, s32[4]{0:T(128)}, u32[]{:S(2)}) copy-start(s32[4]{0:T(128)} %param.10) | copy-start | bytes 52
  2.4 7.3 %copy-start.3 = (s32[4]{0:T(128)S(1)}, s32[4]{0:T(128)}, u32[]{:S(2)}) copy-start(s32[4]{0:T(128)} %param.11) | copy-start | bytes 52
  2.4 44.0 %copy-start = (f32[8,3072]{1,0:T(8,128)S(1)}, f32[8,3072]{1,0:T(8,128)}, u32[]{:S(2)}) copy-start(f32[8,3072]{1,0:T(8,128)} %gate_ref.1) | copy-start | bytes 294916
  2.4 44.0 %all-to-all-start = ((bf16[32,3,64,128]{3,2,1,0:T(8,128)(2,1)}), bf16[32,3,64,128]{3,2,1,0:T(8,128)(2,1)S(1)}, u32[]{:S(2)}, u32[]{:S(2)}) async-start(bf16[32,3,64,128]{3,2,1,0:T(8,128)(2,1)} %pack.1), calls=%async_computation | async-start | bytes 3145728 | tf_op jit(solution)/shard_map/all_to_all | solution.py:264

commit v6 on v4

--- a/solution.py
+++ b/solution.py
@@ -100,7 +100,11 @@
 def pack_kernel(parts, held, q_ref, k_ref, v_ref, out_ref, in_buf, out_buf, in_sem, out_sem):
     slots = out_ref.shape[0] // parts
     arrays = (q_ref, k_ref, v_ref)
-    copies = [pltpu.make_async_copy(ref, in_buf.at[i], in_sem.at[i]) for i, ref in enumerate(arrays)]
+    half = q_ref.shape[0] // 2
+    pieces = [(i, pl.ds(r * half, half)) for i in range(len(arrays)) for r in range(2)]
+    copies = [
+        pltpu.make_async_copy(arrays[i].at[r], in_buf.at[i, r], in_sem.at[n]) for n, (i, r) in enumerate(pieces)
+    ]
     for copy in copies:
         copy.start()
     for s in range(held, slots):
@@ -108,13 +112,13 @@
             for i in range(len(arrays)):
                 out_buf[i, p * slots + s] = jnp.zeros(out_buf.shape[2:], out_buf.dtype)
     stores = []
-    for i, copy in enumerate(copies):
-        copy.wait()
+    for n, (i, r) in enumerate(pieces):
+        copies[n].wait()
         for p in range(parts):
             for s in range(held):
                 h = p * held + s
-                out_buf[i, p * slots + s] = in_buf[i, :, h * HEAD_DIM : (h + 1) * HEAD_DIM]
-        stores.append(pltpu.make_async_copy(out_buf.at[i], out_ref.at[:, i], out_sem.at[i]))
+                out_buf[i, p * slots + s, r] = in_buf[i, r, h * HEAD_DIM : (h + 1) * HEAD_DIM]
+        stores.append(pltpu.make_async_copy(out_buf.at[i, :, r], out_ref.at[:, i, r], out_sem.at[n]))
         stores[-1].start()
     for store in stores:
         store.wait()
@@ -131,8 +135,8 @@
         scratch_shapes=[
             pltpu.VMEM((count, local, feat), jnp.bfloat16),
             pltpu.VMEM((count, n_dev, local, HEAD_DIM), jnp.bfloat16),
-            pltpu.SemaphoreType.DMA((count,)),
-            pltpu.SemaphoreType.DMA((count,)),
+            pltpu.SemaphoreType.DMA((2 * count,)),
+            pltpu.SemaphoreType.DMA((2 * count,)),
         ],
         compiler_params=pltpu.CompilerParams(vmem_limit_bytes=60 * 1024 * 1024),
         name="pack",

time: 72.8 us -> 72.5 us (level)
  no operation moved by 1% of the time
where the time goes in v6:
time: 72.5 us; the launch traced here: 72.9 us
  waiting for transfers between devices  36.7 us (51%)
  blocking collectives  19.9 us (27%)
  Pallas kernels  8.97 us (12%)
  starting transfers between devices  7.1 us (10%)
    all_to_all x1, waiting for transfers between devices, head_each(): got = lax.all_to_all(sent, axes, split_axis=0, concat_axis=0, tiled=True)  36.7 us
    all_to_all x1, blocking collectives, head_each(): back = lax.all_to_all(result, axes, split_axis=0, concat_axis=0, tiled=True)  19.9 us
    all_to_all x1, starting transfers between devices, head_each(): got = lax.all_to_all(sent, axes, split_axis=0, concat_axis=0, tiled=True)  7.1 us
    pallas_call x1, Pallas kernels, head_each(): pl.pallas_call(attention_kernel, out_shape=jax.ShapeDtypeStruct((n_dev, l...  5.92 us
    pallas_call x1, Pallas kernels, pack(): pl.pallas_call(functools.partial(pack_kernel, parts, held), out_shape=jax...  2.32 us
  transfers between devices with their start and end apart: 1, of which 1 were waited for; matrix products, arithmetic and copies ran while one was open for 0% of the time, Pallas kernels for 0%

profile of v6, /device:TPU:1, one launch (start us, length us, event | category | flops | bytes accessed | tf_op | source)
XLA Modules:
  0.0 72.9 jit_solution(5394025403080219643)
XLA Ops:
  0.0 2.3 %pack.1 = bf16[32,3,64,128]{3,2,1,0:T(8,128)(2,1)} custom-call(bf16[64,3072]{1,0:T(8,128)(2,1)} %q_ref.1, bf16[64,3072]{1,0:T(8,128)(2,1)} %k_ref.1, bf16[64,3072]{1,0:T(8,128)(2,1)} %v_ref.1), custom_call_target="tpu_custom_call" | custom-call | tf_op jit(solution)/shard_map/pack/pallas_call | solution.py:130
  2.3 0.0 copy-start.1
  2.3 0.0 copy-start.2
  2.4 0.0 copy-start.3
  2.4 0.0 copy-start
  2.4 7.1 %all-to-all-start = ((bf16[32,3,64,128]{3,2,1,0:T(8,128)(2,1)}), bf16[32,3,64,128]{3,2,1,0:T(8,128)(2,1)S(1)}, u32[]{:S(2)}, u32[]{:S(2)}) async-start(bf16[32,3,64,128]{3,2,1,0:T(8,128)(2,1)} %pack.1), calls=%async_computation | async-start | bytes 3145728 | tf_op jit(solution)/shard_map/all_to_all | solution.py:268
  9.5 0.0 copy-done.1
  9.5 0.1 reshape.3
  9.6 0.0 copy-done.2
  9.6 0.0 copy-done.3
  9.6 0.1 concatenate.3.info_ref
  9.7 36.7 %all-to-all-done.got_ref = bf16[32,3,64,128]{3,2,1,0:T(8,128)(2,1)S(1)} async-done(((bf16[32,3,64,128]{3,2,1,0:T(8,128)(2,1)}), bf16[32,3,64,128]{3,2,1,0:T(8,128)(2,1)S(1)}, u32[]{:S(2)}, u32[]{:S(2)}) %all-to-all-start) | async-done | bytes 1572896 | tf_op jit(solution)/shard_map/all_to_all | solution.py:268
  46.3 0.0 copy-done
  46.3 5.9 %attention.1 = bf16[32,64,128]{2,1,0:T(8,128)(2,1)S(1)} custom-call(s32[26]{0:T(128)S(1)} %concatenate.3.info_ref, bf16[32,3,64,128]{3,2,1,0:T(8,128)(2,1)S(1)} %all-to-all-done.got_ref, f32[8,3072]{1,0:T(8,128)S(1)} %copy-done), custom_call_target="tpu_custom_call" | custom-call | tf_op jit(solution)/shard_map/attention/pallas_call | solution.py:270
  52.3 19.9 %all_to_all.10.in_ref = bf16[32,64,128]{2,1,0:T(8,128)(2,1)S(1)} all-to-all(bf16[32,64,128]{2,1,0:T(8,128)(2,1)S(1)} %attention.1), channel_id=1, replica_groups=mesh['seq'=16,'head'=2] {'seq','head'}, dimensions={0} | all-to-all | bytes 1048576 | tf_op jit(solution)/shard_map/all_to_all | solution.py:287
  72.1 0.7 %unpack.1 = bf16[64,3072]{1,0:T(8,128)(2,1)} custom-call(bf16[32,64,128]{2,1,0:T(8,128)(2,1)S(1)} %all_to_all.10.in_ref), custom_call_target="tpu_custom_call" | custom-call | tf_op jit(solution)/shard_map/unpack/pallas_call | solution.py:288
Async XLA Ops:
  2.3 7.2 %copy-start.1 = (s32[4,4]{1,0:T(4,128)S(1)}, s32[4,4]{1,0:T(4,128)}, u32[]{:S(2)}) copy-start(s32[4,4]{1,0:T(4,128)} %param.12) | copy-start | bytes 196
  2.3 7.3 %copy-start.2 = (s32[4]{0:T(128)S(1)}, s32[4]{0:T(128)}, u32[]{:S(2)}) copy-start(s32[4]{0:T(128)} %param.10) | copy-start | bytes 52
  2.4 7.3 %copy-start.3 = (s32[4]{0:T(128)S(1)}, s32[4]{0:T(128)}, u32[]{:S(2)}) copy-start(s32[4]{0:T(128)} %param.11) | copy-start | bytes 52
  2.4 44.0 %copy-start = (f32[8,3072]{1,0:T(8,128)S(1)}, f32[8,3072]{1,0:T(8,128)}, u32[]{:S(2)}) copy-start(f32[8,3072]{1,0:T(8,128)} %gate_ref.1) | copy-start | bytes 294916
  2.4 44.0 %all-to-all-start = ((bf16[32,3,64,128]{3,2,1,0:T(8,128)(2,1)}), bf16[32,3,64,128]{3,2,1,0:T(8,128)(2,1)S(1)}, u32[]{:S(2)}, u32[]{:S(2)}) async-start(bf16[32,3,64,128]{3,2,1,0:T(8,128)(2,1)} %pack.1), calls=%async_computation | async-start | bytes 3145728 | tf_op jit(solution)/shard_map/all_to_all | solution.py:268
